TPU v7x, 256 devices: a whole 4x4x8 slice. The times are simulated.
256 devices in a mesh: dp: 8 (over x, core), context: 32 (over z, y).
Axes of the slice: x: 4, y: 4, z: 8, core: 2. Of those that a mesh axis runs over, the one named last changes fastest.
Arguments:
- queries: bfloat16 [8, 4096, 4096], P('dp', 'context'), may hold values from -75 to 75
- keys: bfloat16 [8, 4096, 512], P('dp', 'context'), may hold values from -75 to 75
- values: bfloat16 [8, 4096, 512], P('dp', 'context'), may hold values from -6 to 6
- prefix_cached_keys: bfloat16 [8, 512, 512], P('dp', 'context'), may hold values from -27 to 27
- prefix_cached_values: bfloat16 [8, 512, 512], P('dp', 'context'), may hold values from -6 to 6
- out_grad: bfloat16 [8, 4096, 4096], P('dp', 'context'), may hold values from -6 to 6
- query_gain: float32 [128], replicated, may hold values from 0.6 to 4.5
- key_gain: float32 [128], replicated, may hold values from 0.6 to 4.5
- lengths: int32 [8, 8], P('dp'), may hold values from 1 to 1024, 4096 in all within a row
- offsets: int32 [8, 8], P('dp'), may hold values from 1 to 128, 512 in all within a row
Outputs:
- attention: bfloat16 [8, 4096, 4096], P('dp', 'context')
- query_grad: bfloat16 [8, 4096, 4096], P('dp', 'context')
- key_grad: bfloat16 [8, 4096, 512], P('dp', 'context')
- value_grad: bfloat16 [8, 4096, 512], P('dp', 'context')
- gain_grads: float32 [2, 128], replicated
Inputs may be any that keep to these rules, and one draw needn't show every extreme that they name: `lengths`: row g splits window g into 8 pieces laid end to end in order; they sum to 4096, and the longest is exactly 1024. `offsets`: row g holds the cached prefix lengths of the 8 documents of window g, laid end to end in order in its cached rows; they sum to 512, and the longest is exactly 128.
All inputs are finite; a program needn't handle non-finite values.
Results may differ from a plain program's by a relative error of at most 0.017.
The roundings to bfloat16 on the way count: a program that leaves them out, or rounds other values in their place, can miss the bound.
Values may be sent and summed in bfloat16 or wider, within the bound.
A program may use at most 128 MiB of HBM per device.

v0:
```python
import math

import jax
import jax.numpy as jnp
from jax import lax
from jax.sharding import PartitionSpec as P

EPSILON = 1e-06
ROPE_BASE = 1000000.0


def piece_layout(piece_lengths, prefix_lengths, length_total):
    piece_ends = jnp.cumsum(piece_lengths)
    piece_starts = piece_ends - piece_lengths
    token_index = jnp.arange(length_total, dtype=jnp.int32)
    pieces = jnp.sum((token_index[:, None] >= piece_ends[None, :]).astype(jnp.int32), axis=1)
    one_hot = (
        pieces[:, None] == jnp.arange(piece_lengths.shape[0], dtype=jnp.int32)[None, :]
    ).astype(jnp.int32)
    piece_first = jnp.sum(one_hot * piece_starts[None, :], axis=1)
    prefix_rows = jnp.sum(one_hot * prefix_lengths[None, :], axis=1)
    positions = prefix_rows + token_index - piece_first
    return (pieces, positions)


def cache_pieces(prefix_lengths, length_total):
    piece_ends = jnp.cumsum(prefix_lengths)
    token_index = jnp.arange(length_total, dtype=jnp.int32)
    return jnp.sum((token_index[:, None] >= piece_ends[None, :]).astype(jnp.int32), axis=1)


def rotate_normed(projected, scale_factor, positions):
    head_width = projected.shape[-1]
    half_width = head_width // 2
    normed = (
        projected
        * lax.rsqrt(jnp.mean(projected * projected, axis=-1, keepdims=True) + EPSILON)
        * scale_factor
    )
    frequency = jnp.exp(
        jnp.arange(half_width, dtype=jnp.float32) * (-2.0 * math.log(ROPE_BASE) / head_width)
    )
    angles = positions.astype(jnp.float32)[:, None] * frequency[None, :]
    cosine = jnp.cos(angles)[:, None, :]
    sine_part = jnp.sin(angles)[:, None, :]
    first_half = normed[..., :half_width]
    second_half = normed[..., half_width:]
    return jnp.concatenate(
        [
            first_half * cosine - second_half * sine_part,
            second_half * cosine + first_half * sine_part,
        ],
        axis=-1,
    )


def attend_blocks(
    query_heads, grad_heads, key_window, value_window, key_cache, value_cache, pieces, cached
):
    window = query_heads.shape[0]
    head_size = query_heads.shape[2]
    block_rows = min(512, window)
    key_reach = min(window, block_rows + window // 4)
    cache_total = key_cache.shape[0]
    score_scale = 1.0 / math.sqrt(head_size)
    block_count = window // block_rows

    def block_step(carried, block_index):
        key_total, value_total = carried
        block_first = block_index * block_rows
        key_start = jnp.clip(block_first - window // 4, 0, window - key_reach)
        query_block = lax.dynamic_slice_in_dim(query_heads, block_first, block_rows, 0)
        grad_block = lax.dynamic_slice_in_dim(grad_heads, block_first, block_rows, 0)
        key_near = lax.dynamic_slice_in_dim(key_window, key_start, key_reach, 0)
        value_near = lax.dynamic_slice_in_dim(value_window, key_start, key_reach, 0)
        key_row_block = jnp.concatenate([key_cache, key_near], axis=0)
        value_row_block = jnp.concatenate([value_cache, value_near], axis=0)
        query_piece = lax.dynamic_slice_in_dim(pieces, block_first, block_rows, 0)
        key_piece = lax.dynamic_slice_in_dim(pieces, key_start, key_reach, 0)
        query_index = block_first + jnp.arange(block_rows, dtype=jnp.int32)
        key_index = key_start + jnp.arange(key_reach, dtype=jnp.int32)
        near_allowed = (key_piece[None, :] == query_piece[:, None]) & (
            key_index[None, :] <= query_index[:, None]
        )
        allowed = jnp.concatenate([cached[None, :] == query_piece[:, None], near_allowed], axis=1)
        scores = (
            jnp.einsum(
                "qhd,kd->hqk", query_block, key_row_block, preferred_element_type=jnp.float32
            )
            * score_scale
        )
        scores = jnp.where(allowed[None], scores, -jnp.inf)
        row_max = jnp.max(scores, axis=2, keepdims=True)
        weights = jnp.exp(scores - row_max)
        prob_full = weights / jnp.sum(weights, axis=2, keepdims=True)
        prob_low = prob_full.astype(jnp.bfloat16)
        attention = jnp.einsum(
            "hqk,kd->qhd", prob_low, value_row_block, preferred_element_type=jnp.float32
        ).astype(jnp.bfloat16)
        grad_prob = jnp.einsum(
            "qhd,kd->hqk", grad_block, value_row_block, preferred_element_type=jnp.float32
        )
        grad_score = prob_full * (grad_prob - jnp.sum(prob_full * grad_prob, axis=2, keepdims=True))
        grad_low = grad_score.astype(jnp.bfloat16)
        query_grad = (
            jnp.einsum("hqk,kd->qhd", grad_low, key_row_block, preferred_element_type=jnp.float32)
            * score_scale
        ).astype(jnp.bfloat16)
        key_part = (
            jnp.einsum(
                "hqk,qhd->kd",
                grad_low[:, :, cache_total:],
                query_block,
                preferred_element_type=jnp.float32,
            )
            * score_scale
        )
        value_part = jnp.einsum(
            "hqk,qhd->kd",
            prob_low[:, :, cache_total:],
            grad_block,
            preferred_element_type=jnp.float32,
        )
        key_total = lax.dynamic_update_slice_in_dim(
            key_total,
            lax.dynamic_slice_in_dim(key_total, key_start, key_reach, 0) + key_part,
            key_start,
            0,
        )
        value_total = lax.dynamic_update_slice_in_dim(
            value_total,
            lax.dynamic_slice_in_dim(value_total, key_start, key_reach, 0) + value_part,
            key_start,
            0,
        )
        return ((key_total, value_total), (attention, query_grad))

    empty_sum = jnp.zeros((window, head_size), jnp.float32)
    (key_total, value_total), (attention, query_grad) = lax.scan(
        block_step, (empty_sum, empty_sum), jnp.arange(block_count, dtype=jnp.int32)
    )
    return (attention.reshape(window, -1), query_grad.reshape(window, -1), key_total, value_total)


def body(
    queries,
    keys,
    values,
    prefix_cached_keys,
    prefix_cached_values,
    out_grad,
    query_gain,
    key_gain,
    lengths,
    offsets,
):
    devices = lax.axis_size("context")
    own_rank = lax.axis_index("context")
    row_count = queries.shape[1]
    head_size = query_gain.shape[0]
    query_count = queries.shape[2] // head_size
    key_count = keys.shape[2] // head_size
    window = row_count * devices
    cache_total = prefix_cached_keys.shape[1] * devices
    local_heads = query_count // devices
    head_replicas = devices // key_count
    own_slot = own_rank // head_replicas
    pieces, positions = piece_layout(lengths[0], offsets[0], window)
    cached = cache_pieces(offsets[0], cache_total)
    own_positions = lax.dynamic_slice_in_dim(positions, own_rank * row_count, row_count, 0)
    query_pre = queries[0].astype(jnp.float32).reshape(row_count, query_count, head_size)
    query_full, query_pull = jax.vjp(
        lambda tensor, scale_factor: rotate_normed(tensor, scale_factor, own_positions),
        query_pre,
        query_gain,
    )
    query_rot = query_full.astype(jnp.bfloat16).reshape(1, row_count, query_count * head_size)
    key_before_norm = keys[0].astype(jnp.float32).reshape(row_count, key_count, head_size)
    key_full, key_pull = jax.vjp(
        lambda tensor, scale_factor: rotate_normed(tensor, scale_factor, own_positions),
        key_before_norm,
        key_gain,
    )
    key_rotated = key_full.astype(jnp.bfloat16).reshape(1, row_count, key_count * head_size)
    query_heads, grad_heads = (
        lax.all_to_all(query_rot, "context", split_axis=2, concat_axis=1, tiled=True),
        lax.all_to_all(out_grad, "context", split_axis=2, concat_axis=1, tiled=True),
    )
    query_heads = query_heads[0].reshape(window, local_heads, head_size)
    grad_heads = grad_heads[0].reshape(window, local_heads, head_size)
    key_all, value_all, key_old, value_old = (
        lax.all_gather(key_rotated, "context", axis=1, tiled=True),
        lax.all_gather(values, "context", axis=1, tiled=True),
        lax.all_gather(prefix_cached_keys, "context", axis=1, tiled=True),
        lax.all_gather(prefix_cached_values, "context", axis=1, tiled=True),
    )

    def own_columns(tensor):
        return lax.dynamic_slice_in_dim(tensor[0], own_slot * head_size, head_size, 1)

    key_window = own_columns(key_all)
    value_window = own_columns(value_all)
    key_cache = own_columns(key_old)
    value_cache = own_columns(value_old)
    attention, query_grad, key_total, value_total = attend_blocks(
        query_heads, grad_heads, key_window, value_window, key_cache, value_cache, pieces, cached
    )
    attention_rows, query_rows = (
        lax.all_to_all(
            attention.reshape(1, window, -1), "context", split_axis=1, concat_axis=2, tiled=True
        ),
        lax.all_to_all(
            query_grad.reshape(1, window, -1), "context", split_axis=1, concat_axis=2, tiled=True
        ),
    )
    head_pick = (jnp.arange(key_count, dtype=jnp.int32) == own_slot).astype(jnp.float32)

    def place_head(total):
        return (head_pick[None, :, None] * total[:, None, :]).reshape(window, key_count * head_size)

    key_gradient_sum, value_gradient_sum = (
        lax.psum_scatter(
            place_head(key_total).astype(jnp.bfloat16), "context", scatter_dimension=0, tiled=True
        ).astype(jnp.float32),
        lax.psum_scatter(
            place_head(value_total).astype(jnp.bfloat16), "context", scatter_dimension=0, tiled=True
        ).astype(jnp.float32),
    )
    key_gradient_sum = key_gradient_sum.reshape(row_count, key_count, head_size)
    value_gradient_sum = value_gradient_sum.reshape(row_count, key_count, head_size)
    query_back = query_rows[0].astype(jnp.float32).reshape(row_count, query_count, head_size)
    query_pre_grad, query_gain_part = query_pull(query_back)
    key_before_norm_gradient, key_gain_part = key_pull(key_gradient_sum)
    gain_grads = lax.psum(jnp.stack([query_gain_part, key_gain_part]), ("dp", "context"))
    return (
        attention_rows,
        query_pre_grad.astype(jnp.bfloat16).reshape(1, row_count, query_count * head_size),
        key_before_norm_gradient.astype(jnp.bfloat16).reshape(1, row_count, key_count * head_size),
        value_gradient_sum.astype(jnp.bfloat16).reshape(1, row_count, key_count * head_size),
        gain_grads,
    )


def solution(mesh):
    in_specs = (
        P("dp", "context", None),
        P("dp", "context", None),
        P("dp", "context", None),
        P("dp", "context", None),
        P("dp", "context", None),
        P("dp", "context", None),
        P(),
        P(),
        P("dp", None),
        P("dp", None),
    )
    out_specs = (
        P("dp", "context", None),
        P("dp", "context", None),
        P("dp", "context", None),
        P("dp", "context", None),
        P(),
    )
    return jax.shard_map(body, mesh=mesh, in_specs=in_specs, out_specs=out_specs, check_vma=False)
```

profile of v0, /device:TPU:1, one launch (start us, length us, event | category | flops | bytes accessed | tf_op | source)
XLA Modules:
  0.0 907.4 jit_solution(15270919100979886388)
XLA Ops:
  16.7 16.7 %copy.118 = bf16[1,128,4096]{1,0,2:T(2,128)(2,1)S(1)} copy(bf16[1,128,4096]{1,2,0:T(8,128)(2,1)S(1)} %bitcast.180) | data formatting | bytes 2097152 | tf_op jit(solution)/shard_map/convert_element_type | solution.py:177
  33.9 23.3 %reduce.12 = bf16[4096,128]{1,0:T(8,128)(2,1)} reduce(bf16[4096,1,128]{2,1,0:T(2,128)(2,1)S(1)} %bitcast.174, bf16[]{:T(256)} %broadcast.186), dimensions={1}, to_apply=%bitcast.138.reduce_sub_computation | reduce | bytes 2097154
  59.4 12.7 %all-to-all-start = ((bf16[32,2,8192]{2,1,0:T(2,128)(2,1)}), bf16[32,2,8192]{2,1,0:T(2,128)(2,1)}, u32[]{:S(2)}, u32[]{:S(2)}) async-start(bf16[32,2,8192]{2,1,0:T(2,128)(2,1)} %reshape.315), calls=%async_computation | async-start | bytes 2097152 | tf_op jit(solution)/shard_map/all_to_all | solution.py:186
  72.1 5.1 copy.89
  77.1 23.3 %reduce.13 = bf16[4096,128]{1,0:T(8,128)(2,1)} reduce(bf16[4096,1,128]{2,1,0:T(2,128)(2,1)S(1)} %bitcast.177, bf16[]{:T(256)} %broadcast.186), dimensions={1}, to_apply=%bitcast.123.reduce_sub_computation | reduce | bytes 2097154
  102.6 8.8 all-to-all-done
  111.4 5.0 all-to-all-start.1
  117.4 58.7 %all_gather.13 = bf16[1,512,512]{2,1,0:T(8,128)(2,1)S(1)} all-gather(bf16[1,16,512]{2,1,0:T(8,128)(2,1)S(1)} %copy-done.21), channel_id=1, replica_groups=mesh['dp'=8,'context'=32] {'context'}, dimensions={1}, use_global_device_ids=true | all-gather | bytes 540672 | tf_op jit(solution)/shard_map/all_gather | solution.py:194
  176.1 38.7 %all_gather.15 = bf16[1,512,512]{2,1,0:T(8,128)(2,1)S(1)} all-gather(bf16[1,16,512]{2,1,0:T(8,128)(2,1)S(1)} %copy-done.22), channel_id=1, replica_groups=mesh['dp'=8,'context'=32] {'context'}, dimensions={1}, use_global_device_ids=true | all-gather | bytes 540672 | tf_op jit(solution)/shard_map/all_gather | solution.py:195
  216.2 4.3 reshape.316
  223.9 4.3 reshape.318
  239.1 183.6 %while.18 = (s32[]{:T(128)}, f32[4096,128]{1,0:T(8,128)}, f32[4096,128]{1,0:T(8,128)}, bf16[8,512,1,128]{3,1,0,2:T(8,128)(2,1)}, bf16[8,512,1,128]{3,1,0,2:T(8,1...) while((s32[]{:T(128)}, f32[4096,128]{1,0:T(8,128)}, ...), condition=%wide.region_12.13_spmd, body=%wide.region_8.12_spmd.sunk | while | flops 1500774912 | bytes 50666160 | solution.py:139
  254.4 3.5 dynamic_update_slice.32
  277.5 3.5 dynamic_update_slice.32
  300.6 3.5 dynamic_update_slice.32
  323.7 3.5 dynamic_update_slice.32
  346.7 3.5 dynamic_update_slice.32
  350.3 3.5 dynamic_update_slice.31
  369.8 3.5 dynamic_update_slice.32
  392.9 3.5 dynamic_update_slice.32
  396.4 3.5 dynamic_update_slice.31
  427.6 4.7 fusion.43
  436.1 23.3 %reduce.15 = bf16[4096,128]{1,0:T(8,128)(2,1)} reduce(bf16[4096,1,128]{2,1,0:T(2,128)(2,1)S(1)} %bitcast.176, bf16[]{:T(256)} %broadcast.186), dimensions={1}, to_apply=%bitcast.136.reduce_sub_computation | reduce | bytes 2097154
  461.6 6.7 all-to-all-start.3
  471.6 23.3 %reduce.14 = bf16[4096,128]{1,0:T(8,128)(2,1)} reduce(bf16[4096,1,128]{2,1,0:T(2,128)(2,1)S(1)} %bitcast.175, bf16[]{:T(256)} %broadcast.186), dimensions={1}, to_apply=%bitcast.137.reduce_sub_computation | reduce | bytes 2097154
  497.0 9.5 %all-to-all-start.2 = ((bf16[32,2,8192]{2,1,0:T(2,128)(2,1)}), bf16[32,2,8192]{2,1,0:T(2,128)(2,1)}, u32[]{:S(2)}, u32[]{:S(2)}) async-start(bf16[32,2,8192]{2,1,0:T(2,128)(2,1)} %reshape.319), calls=%async_computation.2 | async-start | bytes 2097152 | tf_op jit(solution)/shard_map/all_to_all | solution.py:209
  506.5 4.3 reshape.322
  517.0 9.3 %all-to-all-done.2 = bf16[32,2,8192]{2,1,0:T(2,128)(2,1)} async-done(((bf16[32,2,8192]{2,1,0:T(2,128)(2,1)}), bf16[32,2,8192]{2,1,0:T(2,128)(2,1)}, u32[]{:S(2)}, u32[]{:S(2)}) %all-to-all-start.2) | async-done | bytes 1048608 | tf_op jit(solution)/shard_map/all_to_all | solution.py:209
  526.3 4.3 reshape.320
  532.8 144.0 %reduce-scatter.3.cloned.1.call-done = bf16[128,512]{1,0:T(8,128)(2,1)} async-done(((bf16[4096,512]{1,0:T(8,128)(2,1)}), bf16[128,512]{1,0:T(8,128)(2,1)}) %reduce-scatter.3.cloned.1.call-update) | async-done | bytes 131088 | tf_op jit(solution)/shard_map/reduce_scatter | solution.py:222
  680.0 79.9 %psum.7 = f32[2,128]{1,0:T(2,128)} all-reduce(f32[2,128]{1,0:T(2,128)S(1)} %pad_maximum_fusion.8), channel_id=1, replica_groups=mesh['dp'=8,'context'=32] {'dp','context'}, use_global_device_ids=true, to_apply=%region_19.20 | all-reduce | flops 256 | bytes 2048 | tf_op jit(solution)/shard_map/psum | solution.py:234
  759.9 140.5 %reduce-scatter.5.cloned.1.call-done = bf16[128,512]{1,0:T(8,128)(2,1)} async-done(((bf16[4096,512]{1,0:T(8,128)(2,1)}), bf16[128,512]{1,0:T(8,128)(2,1)}) %reduce-scatter.5.cloned.1.call-update) | async-done | bytes 131088 | tf_op jit(solution)/shard_map/reduce_scatter | solution.py:225
  (350 shorter events, 204.0 us)
Async XLA Ops:
  7.2 7.7 copy-start.2
  7.2 224.5 %all-gather.5.cloned.1.call-start = ((), (), s32[]{:S(2)}) async-start(), calls=%async_computation.7 | async-start | bytes 4325376 | tf_op jit(solution)/shard_map/all_gather | solution.py:193
  7.9 226.0 %all-gather.3.cloned.1.call-start = ((), (), s32[]{:S(2)}) async-start(), calls=%async_computation.6 | async-start | bytes 4325376 | tf_op jit(solution)/shard_map/all_gather | solution.py:192
  59.4 52.1 %all-to-all-start = ((bf16[32,2,8192]{2,1,0:T(2,128)(2,1)}), bf16[32,2,8192]{2,1,0:T(2,128)(2,1)}, u32[]{:S(2)}, u32[]{:S(2)}) async-start(bf16[32,2,8192]{2,1,0:T(2,128)(2,1)} %reshape.315), calls=%async_computation | async-start | bytes 2097152 | tf_op jit(solution)/shard_map/all_to_all | solution.py:186
  100.4 16.1 %copy-start.27 = (s32[1,8]{1,0:T(1,128)S(1)}, s32[1,8]{1,0:T(1,128)}, u32[]{:S(2)}) copy-start(s32[1,8]{1,0:T(1,128)} %param.21) | copy-start | bytes 100
  100.4 17.0 %copy-start.21 = (bf16[1,16,512]{2,1,0:T(8,128)(2,1)S(1)}, bf16[1,16,512]{2,1,0:T(8,128)(2,1)}, u32[]{:S(2)}) copy-start(bf16[1,16,512]{2,1,0:T(8,128)(2,1)} %param.15) | copy-start | bytes 49156
  100.4 75.7 %copy-start.22 = (bf16[1,16,512]{2,1,0:T(8,128)(2,1)S(1)}, bf16[1,16,512]{2,1,0:T(8,128)(2,1)}, u32[]{:S(2)}) copy-start(bf16[1,16,512]{2,1,0:T(8,128)(2,1)} %param.16) | copy-start | bytes 49156
  111.4 112.5 %all-to-all-start.1 = ((bf16[32,2,8192]{2,1,0:T(2,128)(2,1)}), bf16[32,2,8192]{2,1,0:T(2,128)(2,1)}, u32[]{:S(2)}, u32[]{:S(2)}) async-start(bf16[32,2,8192]{2,1,0:T(2,128)(2,1)} %reshape.317), calls=%async_computation.1 | async-start | bytes 2097152 | tf_op jit(solution)/shard_map/all_to_all | solution.py:187
  116.4 560.3 %reduce-scatter.3.cloned.1.call-start = ((), (), s32[]{:S(2)}) async-start(), calls=%async_computation.8 | async-start | bytes 4325376 | tf_op jit(solution)/shard_map/reduce_scatter | solution.py:222
  254.4 7.8 copy-start.18
  254.4 7.8 copy-start.29
  277.5 7.8 copy-start.18
  277.5 7.8 copy-start.29
  300.6 7.8 copy-start.18
  300.6 7.8 copy-start.29
  323.7 7.8 copy-start.18
  323.7 7.7 copy-start.29
  346.7 7.7 copy-start.18
  346.7 7.7 copy-start.29
  369.8 7.7 copy-start.18
  369.8 7.7 copy-start.29
  392.9 7.8 copy-start.18
  392.9 7.8 copy-start.29
  416.0 6.7 copy-start.18
  432.4 468.1 %reduce-scatter.5.cloned.1.call-start = ((), (), s32[]{:S(2)}) async-start(), calls=%async_computation.9 | async-start | bytes 4325376 | tf_op jit(solution)/shard_map/reduce_scatter | solution.py:225
  461.6 35.4 %all-to-all-start.3 = ((bf16[32,2,8192]{2,1,0:T(2,128)(2,1)}), bf16[32,2,8192]{2,1,0:T(2,128)(2,1)}, u32[]{:S(2)}, u32[]{:S(2)}) async-start(bf16[32,2,8192]{2,1,0:T(2,128)(2,1)} %reshape.321), calls=%async_computation.3 | async-start | bytes 2097152 | tf_op jit(solution)/shard_map/all_to_all | solution.py:212
  497.0 29.3 %all-to-all-start.2 = ((bf16[32,2,8192]{2,1,0:T(2,128)(2,1)}), bf16[32,2,8192]{2,1,0:T(2,128)(2,1)}, u32[]{:S(2)}, u32[]{:S(2)}) async-start(bf16[32,2,8192]{2,1,0:T(2,128)(2,1)} %reshape.319), calls=%async_computation.2 | async-start | bytes 2097152 | tf_op jit(solution)/shard_map/all_to_all | solution.py:209
  530.8 147.0 %copy-start.6 = (f32[128,64]{1,0:T(8,128)S(1)}, f32[128,64]{1,0:T(8,128)}, u32[]{:S(2)}) copy-start(f32[128,64]{1,0:T(8,128)} %copy-done.5) | copy-start | bytes 98308
  530.8 147.0 %copy-start.8 = (f32[128,64]{1,0:T(8,128)S(1)}, f32[128,64]{1,0:T(8,128)}, u32[]{:S(2)}) copy-start(f32[128,64]{1,0:T(8,128)} %copy-done.7) | copy-start | bytes 98308
  531.5 146.6 %copy-start.4 = (f32[128,4]{1,0:T(8,128)S(1)}, f32[128,4]{1,0:T(8,128)}, u32[]{:S(2)}) copy-start(f32[128,4]{1,0:T(8,128)} %copy-done.3) | copy-start | bytes 6148
  531.5 146.6 %copy-start.24 = (f32[128]{0:T(128)S(1)}, f32[128]{0:T(128)}, u32[]{:S(2)}) copy-start(f32[128]{0:T(128)} %param.19) | copy-start | bytes 1540
  531.5 147.1 %copy-start.20 = (f32[128,4]{0,1:T(4,128)S(1)}, f32[128,4]{0,1:T(4,128)}, u32[]{:S(2)}) copy-start(f32[128,4]{0,1:T(4,128)} %copy-done.19) | copy-start | bytes 6148
  (27 other events, 58.5 us)
Sparse Core Ops, SparseCore 0:
  10.6 102.6 all-gather.4
  116.4 80.6 all-gather.2
  432.5 244.2 reduce-scatter.2
  681.6 218.7 reduce-scatter.4
where the time goes:
time: 922 us; the launch traced here: 907 us
  waiting for transfers between devices  304 us (33%)
  blocking collectives  177 us (19%)
  local copies, waits for them, and re-layouts  173 us (19%)
  other arithmetic  133 us (14%)
  matrix products  65 us (7%)
  starting transfers between devices  34.3 us (4%)
  between operations  14.9 us (2%)
    reduce_scatter x1, waiting for transfers between devices, body(): lax.psum_scatter(place_head(key_total).astype(jnp.bfloat16), 'context', s...  144 us
    reduce_scatter x1, waiting for transfers between devices, body(): lax.psum_scatter(place_head(value_total).astype(jnp.bfloat16), 'context',...  141 us
    unnamed x4, other arithmetic  93.2 us
    psum x1, blocking collectives, body(): lax.psum(jnp.stack([query_gain_part, key_gain_part]), ('dp', 'context'))  79.9 us
    all_gather x1, blocking collectives, body(): lax.all_gather(prefix_cached_keys, 'context', axis=1, tiled=True)  58.7 us
    all_gather x1, blocking collectives, body(): lax.all_gather(prefix_cached_values, 'context', axis=1, tiled=True)  38.7 us
    unnamed x70, local copies, waits for them, and re-layouts  38 us
    dynamic_update_slice x8, local copies, waits for them, and re-layouts, block_step(): lax.dynamic_update_slice_in_dim(value_total, lax.dynamic_slice_in_dim(val...  27.7 us
  transfers between devices with their start and end apart: 8, of which 4 were waited for; matrix products, arithmetic and copies ran while one was open for 20% of the time, Pallas kernels for 0%

commit v1 on v0

v1 whole, which is shorter than its diff:
```python
import functools
import math

import jax
import jax.numpy as jnp
from jax import lax
from jax.experimental import pallas as pl
from jax.experimental.pallas import tpu as pltpu
from jax.sharding import PartitionSpec as P

EPSILON = 1e-06
ROPE_BASE = 1000000.0
D = 128
HALF = D // 2
HQ = 8
NY = 4
NZ = 8
ROWS = 128
SLAB = NY * ROWS
COLS = HQ * D
CACHE = 512
CPART = CACHE // (NY * NZ)
WINDOW = 3 * SLAB
KEYS = CACHE + WINDOW
SEGS = 8
REACH = SLAB * 2 + ROWS
MET = CACHE + REACH
CH = 2
NC = HQ // CH
LANES = CH * D
WIDE = 2 * LANES
TILES = ((0, 512), (512, 512), (1024, 512), (1536, 128))
SCALE = 1.0 / math.sqrt(D)
EXP2_SCALE = SCALE * math.log2(math.e)
MASKED = -1e30
F32 = jnp.float32
BF16 = jnp.bfloat16


def aligned(x, n):
    return x if isinstance(x, int) else pl.multiple_of(x, n)


def place():
    c = lax.axis_index("context")
    return lax.div(c, NY), lax.rem(c, NY)


def remote(src, dst, send, recv, z, y):
    return pltpu.make_async_remote_copy(
        src_ref=src,
        dst_ref=dst,
        send_sem=send,
        recv_sem=recv,
        device_id={"context": z * NY + y},
        device_id_type=pl.DeviceIdType.MESH,
    )


def greet_plane(z, y):
    barrier = pltpu.get_barrier_semaphore()
    for d in range(1, NY):
        pl.semaphore_signal(
            barrier,
            inc=1,
            device_id={"context": z * NY + lax.rem(y + d, NY)},
            device_id_type=pl.DeviceIdType.MESH,
        )
    for d in range(1, NZ):
        pl.semaphore_signal(
            barrier,
            inc=1,
            device_id={"context": lax.rem(z + d, NZ) * NY + y},
            device_id_type=pl.DeviceIdType.MESH,
        )
    return barrier


def rotate(a, b, cos, sin):
    return a * cos - b * sin, b * cos + a * sin


def column(row_ref):
    return jnp.broadcast_to(row_ref[...], (D, D)).T


def norm_forward(xt, gain):
    r = lax.rsqrt(jnp.mean(xt * xt, axis=0, keepdims=True) + EPSILON)
    return xt * r * gain


def norm_backward(xt, gain, dyt, cos, sin):
    r = lax.rsqrt(jnp.mean(xt * xt, axis=0, keepdims=True) + EPSILON)
    xh = xt * r
    d1, d2 = dyt[:HALF], dyt[HALF:]
    dn = jnp.concatenate([d1 * cos + d2 * sin, d2 * cos - d1 * sin], axis=0)
    dxh = dn * gain
    dx = r * (dxh - xh * jnp.mean(dxh * xh, axis=0, keepdims=True))
    return dx, dn * xh


def fetch_pieces(lengths_in, offsets_in, lengths, offsets, sems):
    copies = [
        pltpu.make_async_copy(lengths_in, lengths, sems.at[0]),
        pltpu.make_async_copy(offsets_in, offsets, sems.at[1]),
    ]
    for copy in copies:
        copy.start()
    return copies


def fused_kernel(
    ndp,
    lengths_in,
    offsets_in,
    qgain,
    kgain,
    q,
    g,
    k,
    v,
    pk,
    pv,
    attn_out,
    dq_out,
    kg_out,
    vg_out,
    gains_out,
    qs,
    gs,
    ks,
    vs,
    kt,
    vt,
    kraw,
    kx,
    cos_buf,
    sin_buf,
    gain_buf,
    bias,
    xt,
    qt,
    gt,
    qr,
    gr,
    s_buf,
    gp_buf,
    p_hold,
    ds_hold,
    dk,
    dv,
    gacc,
    oh,
    dqh,
    oa,
    oq,
    okg,
    ovg,
    rk,
    rv,
    dkh,
    dvh,
    kg,
    vg,
    gy,
    gz,
    gx,
    lengths,
    offsets,
    psems,
    ysend,
    yrecv,
    qsend,
    qrecv,
    zsend,
    zrecv,
    nsend,
    nrecv,
    csend,
    crecv,
    osend,
    orecv,
    bsend,
    brecv,
    hsend,
    hrecv,
    gsend,
    grecv,
    local,
    olocal,
):
    z, y = place()
    dp = lax.axis_index("dp")
    pieces = fetch_pieces(lengths_in, offsets_in, lengths, offsets, psems)
    barrier = greet_plane(z, y)
    for d in range(1, ndp):
        pl.semaphore_signal(
            barrier,
            inc=1,
            device_id={"dp": lax.rem(dp + d, ndp)},
            device_id_type=pl.DeviceIdType.MESH,
        )
    after, before = lax.rem(z + 1, NZ), lax.rem(z + NZ - 1, NZ)
    for d in range(1, NY):
        pl.semaphore_signal(
            barrier,
            inc=1,
            device_id={"context": before * NY + lax.rem(y + d, NY)},
            device_id_type=pl.DeviceIdType.MESH,
        )
    pl.semaphore_wait(barrier, NY - 1 + NZ - 1 + ndp - 1 + NY - 1)

    own = CACHE + 2 * SLAB
    crow = z * (NY * CPART)
    hops = (2, 1, 3)

    def parts(head, row):
        one = pl.ds(head * D, D)
        cached = pl.ds(crow + row * CPART, CPART)
        return [
            (k.at[:, one], kraw.at[pl.ds(2 * SLAB + row * ROWS, ROWS), :]),
            (v.at[:, one], vs.at[pl.ds(own + row * ROWS, ROWS), :]),
            (pk.at[:, one], ks.at[cached, :]),
            (pv.at[:, one], vs.at[cached, :]),
        ]

    mine = [
        pltpu.make_async_copy(src, dst, local.at[i])
        for i, (src, dst) in enumerate(parts(y, y))
    ]
    ycopies = {}
    zcopies = {}

    def send(i):
        for d in hops:
            yt = lax.rem(y + d, NY)
            src, dst = parts(yt, y)[i]
            copy = remote(src, dst, ysend.at[i, d - 1], yrecv.at[i, d - 1], z, yt)
            copy.start()
            ycopies[i, d] = copy
        mine[i].start()

    def arrived(i):
        mine[i].wait()
        for d in hops:
            ycopies[i, d].wait_recv()

    def send_after(j):
        buf, top = ((kraw, SLAB), (vs, own - SLAB))[j]
        for d in range(NY):
            yt = lax.rem(y + d, NY)
            copy = remote(
                parts(yt, y)[j][0],
                buf.at[pl.ds(top + y * ROWS, ROWS), :],
                nsend.at[j, d],
                nrecv.at[j, d],
                after,
                yt,
            )
            copy.start()
            zcopies[j, d, "next"] = copy

    for j in range(2):
        send_after(j)
    for i in (2, 3, 0, 1):
        send(i)

    whole = pl.ds(y * COLS, COLS)
    here = pl.ds(y * ROWS, ROWS)
    mine_q = [
        pltpu.make_async_copy(x.at[:, whole], buf.at[here, :], local.at[4 + a])
        for a, (x, buf) in enumerate(((q, qs), (g, gs)))
    ]

    def query_copies(w, d):
        yt = lax.rem(y + d, NY)
        return [
            remote(
                x.at[:, pl.ds(yt * COLS + w * WIDE, WIDE)],
                buf.at[here, pl.ds(w * WIDE, WIDE)],
                qsend.at[a, w, d - 1],
                qrecv.at[a, w, d - 1],
                z,
                yt,
            )
            for a, (x, buf) in enumerate(((q, qs), (g, gs)))
        ]

    def send_queries(ways):
        for w, d in ways:
            for copy in query_copies(w, d):
                copy.start()

    for copy in mine_q:
        copy.start()
    send_queries(((0, 3), (0, 1)))

    for copy in pieces:
        copy.wait()

    def per_token(t):
        first = run = jnp.int32(0)
        low = jnp.zeros_like(t)
        clo = jnp.zeros_like(t)
        chi = jnp.zeros_like(t)
        for s in range(SEGS):
            end = first + lengths[0, s]
            stop = run + offsets[0, s]
            inside = (t >= first) & (t < end)
            low = jnp.where(inside, first, low)
            clo = jnp.where(inside, run, clo)
            chi = jnp.where(inside, stop, chi)
            first, run = end, stop
        return low, clo, chi

    t = (z - 2) * SLAB + lax.broadcasted_iota(jnp.int32, (1, WINDOW), 1)
    low, clo, chi = per_token(t)
    frequency = jnp.exp(
        lax.broadcasted_iota(jnp.int32, (HALF, 1), 0).astype(F32)
        * (-2.0 * math.log(ROPE_BASE) / D)
    )
    angles = frequency * (t - low + chi - clo).astype(F32)

    def forward(j):
        x, top = ((kraw, SLAB), (vs, own - SLAB))[j]
        copy = remote(
            x.at[pl.ds(top, SLAB), :],
            x.at[pl.ds(top - SLAB, SLAB), :],
            zsend.at[j],
            zrecv.at[j],
            after,
            y,
        )
        copy.start()
        zcopies[j, "far"] = copy

    kgain_col = column(kgain)[:, :1]

    def rotate_keys(slab):
        rows = slice(slab * SLAB, (slab + 1) * SLAB)
        met = slice(CACHE + slab * SLAB, CACHE + (slab + 1) * SLAB)
        x = kraw[rows, :].T.astype(F32)
        xh = x * lax.rsqrt(jnp.mean(x * x, axis=0, keepdims=True) + EPSILON)
        kx[:, rows] = xh
        n = xh * kgain_col
        a, b = rotate(n[:HALF], n[HALF:], cos_buf[:, rows], sin_buf[:, rows])
        rotated = jnp.concatenate([a, b], axis=0).astype(BF16)
        kt[:, met] = rotated
        ks[met, :] = rotated.T

    cos_buf[...] = jnp.cos(angles)
    sin_buf[...] = jnp.sin(angles)
    gain_buf[...] = column(qgain)
    def cached_to(j, i, rows, d):
        part = (ks, vs)[j].at[rows, :]
        zt = lax.rem(z + d, NZ)
        copy = remote(part, part, csend.at[j, i], crecv.at[j, i], zt, y)
        copy.start()
        zcopies[j, i, "cached"] = copy

    for j in range(2):
        arrived(2 + j)
        for i, d in enumerate((1, 2, 5, 6, 7)):
            cached_to(j, i, pl.ds(crow, NY * CPART), d)
    for j in range(2):
        for d in range(NY):
            zcopies[j, d, "next"].wait_recv()
        forward(j)
    send_queries(((1, 3), (1, 1), (0, 2), (1, 2)))

    def mask(b, carry):
        t = z * SLAB + b * ROWS + lax.broadcasted_iota(jnp.int32, (1, ROWS), 1)
        low, clo, chi = per_token(t)
        rows = lax.broadcasted_iota(jnp.int32, (CACHE, ROWS), 0)
        base = aligned(b * MET, ROWS)
        seen = (rows >= clo) & (rows < chi)
        bias[pl.ds(base, CACHE), :] = jnp.where(seen, 0.0, MASKED)
        rows = lax.broadcasted_iota(jnp.int32, (REACH, ROWS), 0)
        token = rows + ((z - 2) * SLAB + b * ROWS)
        seen = (token >= low) & (token <= t)
        base = aligned(b * MET + CACHE, ROWS)
        bias[pl.ds(base, REACH), :] = jnp.where(seen, 0.0, MASKED)
        return carry

    lax.fori_loop(0, NY, mask, 0)
    dk[...] = jnp.zeros_like(dk)
    dv[...] = jnp.zeros_like(dv)
    gacc[...] = jnp.zeros_like(gacc)

    arrived(0)
    rotate_keys(2)
    arrived(1)
    vt[:, own:] = vs[own:, :].T
    for j in range(2):
        zcopies[j, 2, "cached"].wait_recv()
        for i, d in ((5, 7), (6, 6)):
            cached_to(j, i, pl.ds(lax.rem(z + 3, NZ) * (NY * CPART), NY * CPART), d)
    rotate_keys(1)
    vt[:, CACHE + SLAB : own] = vs[CACHE + SLAB : own, :].T

    def spot(w, b, u=0):
        return aligned((w * NY + b) * WIDE + u * LANES, LANES)

    def prepare(w, b):
        rows = pl.ds(aligned(b * ROWS, ROWS), ROWS)
        now = pl.ds(aligned(2 * SLAB + b * ROWS, ROWS), ROWS)
        cos = cos_buf[:, now]
        sin = sin_buf[:, now]
        for h in range(2 * CH):
            cols = pl.ds(aligned(w * WIDE + h * D, D), D)
            lanes = pl.ds(aligned(spot(w, b) + h * D, D), D)
            x = qs[rows, cols].T
            xt[:, lanes] = x
            n = norm_forward(x.astype(F32), gain_buf[...])
            r1, r2 = rotate(n[:HALF], n[HALF:], cos, sin)
            rot = jnp.concatenate([r1, r2], axis=0).astype(BF16)
            qt[:, lanes] = rot
            qr[lanes, :] = rot.T
            grad = gs[rows, cols]
            gr[lanes, :] = grad
            gt[:, lanes] = grad.T

    for copy in mine_q:
        copy.wait()

    for j, (x, xtr) in enumerate(((ks, kt), (vs, vt))):
        for i in range(NZ - 1):
            if i != 2:
                zcopies[j, i, "cached"].wait_recv()
        xtr[:, :CACHE] = x[:CACHE, :].T
    zcopies[0, "far"].wait_recv()
    rotate_keys(0)
    zcopies[1, "far"].wait_recv()
    vt[:, CACHE : CACHE + SLAB] = vs[CACHE : CACHE + SLAB, :].T

    def groups(x):
        return x.reshape(x.shape[0] // 8, 8, LANES)

    sides = range(2)

    def tile(b, first, rows):
        if first < CACHE:
            return pl.ds(first, rows)
        return pl.ds(aligned(first + b * ROWS, ROWS), rows)

    def attend(w, b, held=False):
        lanes = [pl.ds(spot(w, b, u), LANES) for u in sides]
        unit_lanes = pl.ds(spot(w, b), WIDE)

        top = [jnp.full((8, LANES), MASKED, F32) for _ in sides]
        for first, n in TILES:
            at = slice(first, first + n)
            add = bias[pl.ds(aligned(b * MET + first, ROWS), n), :]
            add = jnp.concatenate([add] * CH, axis=1)
            kb = ks[tile(b, first, n), :]
            for u in sides:
                sc = jnp.dot(kb, qt[:, lanes[u]], preferred_element_type=F32)
                sc = sc * EXP2_SCALE + add
                s_buf[u, at, :] = sc
                top[u] = jnp.maximum(top[u], jnp.max(groups(sc), axis=0))
        top = [jnp.max(x, axis=0, keepdims=True) for x in top]
        sums = [jnp.zeros((8, LANES), F32) for _ in sides]
        dots = [jnp.zeros((8, LANES), F32) for _ in sides]
        for first, n in TILES:
            at = slice(first, first + n)
            vb = vs[tile(b, first, n), :]
            for u in sides:
                gp = jnp.dot(vb, gt[:, lanes[u]], preferred_element_type=F32)
                w2 = jnp.exp2(s_buf[u, at, :] - top[u])
                gp_buf[u, at, :] = gp
                sums[u] = sums[u] + jnp.sum(groups(w2), axis=0)
                dots[u] = dots[u] + jnp.sum(groups(w2 * gp), axis=0)
        sums = [jnp.sum(x, axis=0, keepdims=True) for x in sums]
        mean = [jnp.sum(x, axis=0, keepdims=True) / r for x, r in zip(dots, sums)]
        less = [m + jnp.log(x) * math.log2(math.e) for m, x in zip(top, sums)]
        qrow = qr[unit_lanes, :]
        grow = gr[unit_lanes, :]
        ot = [jnp.zeros((D, LANES), F32) for _ in sides]
        dqt = [jnp.zeros((D, LANES), F32) for _ in sides]
        for first, n in TILES:
            at = slice(first, first + n)
            rows = tile(b, first, n)
            probs, grads = [], []
            for u in sides:
                prob = jnp.exp2(s_buf[u, at, :] - less[u])
                ds = (prob * (gp_buf[u, at, :] - mean[u])).astype(BF16)
                prob = prob.astype(BF16)
                if not held:
                    ot[u] += jnp.dot(vt[:, rows], prob, preferred_element_type=F32)
                    dqt[u] += jnp.dot(kt[:, rows], ds, preferred_element_type=F32)
                probs.append(prob)
                grads.append(ds)
            prob = jnp.concatenate(probs, axis=1)
            ds = jnp.concatenate(grads, axis=1)
            if held:
                p_hold[at, :] = prob
                ds_hold[at, :] = ds
            if first >= CACHE:
                dk[rows, :] += jnp.dot(ds, qrow, preferred_element_type=F32)
                dv[rows, :] += jnp.dot(prob, grow, preferred_element_type=F32)
        if not held:
            for u in sides:
                close(w, u, b, ot[u], dqt[u])

    def rest(w, b):
        for u in sides:
            part = slice(u * LANES, (u + 1) * LANES)
            ot = jnp.zeros((D, LANES), F32)
            dqt = jnp.zeros((D, LANES), F32)
            for first, n in TILES:
                at = slice(first, first + n)
                rows = tile(b, first, n)
                ot += jnp.dot(vt[:, rows], p_hold[at, part], preferred_element_type=F32)
                dqt += jnp.dot(kt[:, rows], ds_hold[at, part], preferred_element_type=F32)
            close(w, u, b, ot, dqt)

    def close(w, u, b, ot, dqt):
        here = pl.ds(aligned(b * ROWS, ROWS), ROWS)
        now = pl.ds(aligned(2 * SLAB + b * ROWS, ROWS), ROWS)
        cos = cos_buf[:, now]
        sin = sin_buf[:, now]
        out = ot.astype(BF16)
        back = (dqt * SCALE).astype(BF16).astype(F32)
        for h in range(CH):
            cols = pl.ds(aligned(w * WIDE + u * LANES + h * D, D), D)
            part = slice(h * D, (h + 1) * D)
            oh[here, cols] = out[:, part].T
            x = xt[:, pl.ds(aligned(spot(w, b, u) + h * D, D), D)].astype(F32)
            dx, term = norm_backward(x, gain_buf[...], back[:, part], cos, sin)
            gacc[...] += term
            dqh[here, cols] = dx.astype(BF16).T

    def out_copies(w, d):
        yt = lax.rem(y + d, NY)
        return [
            remote(
                x.at[pl.ds(yt * ROWS, ROWS), pl.ds(w * WIDE, WIDE)],
                buf.at[:, pl.ds(y * COLS + w * WIDE, WIDE)],
                osend.at[a, w, d - 1],
                orecv.at[a, w, d - 1],
                z,
                yt,
            )
            for a, (x, buf) in enumerate(((oh, oa), (dqh, oq)))
        ]

    def out_stays(w):
        return [
            pltpu.make_async_copy(
                x.at[here, pl.ds(w * WIDE, WIDE)],
                buf.at[:, pl.ds(y * COLS + w * WIDE, WIDE)],
                olocal.at[a, w],
            )
            for a, (x, buf) in enumerate(((oh, oa), (dqh, oq)))
        ]

    def step(n, carry):
        w = jnp.where((n == 3) | (n == 4) | (n == 6), 1, 0)
        d = jnp.where(n == 0, 0, jnp.where(n > 4, 2, jnp.where((n == 1) | (n == 3), 1, 3)))
        b = lax.rem(y + d, NY)

        @pl.when(n > 0)
        def _():
            for copy in query_copies(w, NY - d):
                copy.wait_recv()

        prepare(w, b)
        attend(w, b)

        @pl.when(n > 0)
        def _():
            for copy in out_copies(w, d):
                copy.start()

        return carry

    lax.fori_loop(0, 7, step, 0)
    for copy in out_stays(0):
        copy.start()

    half = SLAB // 2
    lower, upper = slice(0, half), slice(half, SLAB)
    sums = ((dk, dkh, rk, SCALE), (dv, dvh, rv, 1.0))

    def back(i, hop, h):
        low, got = sums[i][1], sums[i][2]
        part = pl.ds(h * half, half)
        return remote(
            low.at[h] if hop == 0 else got.at[0, part, :],
            got.at[hop, part, :],
            hsend.at[i, hop, h],
            hrecv.at[i, hop, h],
            before,
            y,
        )

    def first_hop(h):
        for i, (total, low, _, scale) in enumerate(sums):
            rows = slice(CACHE + h * half, CACHE + (h + 1) * half)
            low[h] = (total[rows, :] * scale).astype(BF16)
            back(i, 0, h).start()

    def second_hop(h):
        for i, (total, _, got, scale) in enumerate(sums):
            back(i, 0, h).wait_recv()
            rows = slice(CACHE + SLAB + h * half, CACHE + SLAB + (h + 1) * half)
            at = (lower, upper)[h]
            mid = total[rows, :] * scale + got[0, at, :].astype(F32)
            got[0, at, :] = mid.astype(BF16)
            back(i, 1, h).start()

    prepare(1, y)
    attend(1, y, True)
    first_hop(0)
    first_hop(1)
    rest(1, y)
    for copy in out_stays(1):
        copy.start()
    second_hop(0)

    terms = jnp.zeros((D, ROWS), F32)
    for slab in range(3):
        rows = slice(slab * SLAB, (slab + 1) * SLAB)
        dkt = (dk[CACHE + slab * SLAB : CACHE + (slab + 1) * SLAB, :] * SCALE).T
        a, b = rotate(dkt[:HALF], dkt[HALF:], cos_buf[:, rows], -sin_buf[:, rows])
        term = jnp.concatenate([a, b], axis=0) * kx[:, rows]
        for i in range(SLAB // ROWS):
            terms = terms + term[:, i * ROWS : (i + 1) * ROWS]
    rows = [jnp.sum(x.T, axis=0, keepdims=True) for x in (gacc[...], terms)]
    total = jnp.concatenate(rows + [jnp.zeros((6, D), F32)], axis=0)

    def share(buf, me, n, first, total, device):
        buf[me] = total
        copies = []
        for d in range(1, n):
            copies.append(
                pltpu.make_async_remote_copy(
                    src_ref=buf.at[me],
                    dst_ref=buf.at[me],
                    send_sem=gsend.at[first + d - 1],
                    recv_sem=grecv.at[first + d - 1],
                    device_id=device(lax.rem(me + d, n)),
                    device_id_type=pl.DeviceIdType.MESH,
                )
            )
            copies[-1].start()
        return copies

    def add_up(copies, buf, n):
        for copy in copies:
            copy.wait()
        total = buf[0]
        for i in range(1, n):
            total = total + buf[i]
        return total

    second_hop(1)
    shared = share(gx, dp, ndp, NY + NZ - 2, total, lambda to: {"dp": to})
    kv_out = []

    def leave_row(i, x, buf):
        there = buf.at[:, pl.ds(y * D, D)]
        copies = []
        for d in hops:
            yt = lax.rem(y + d, NY)
            copies.append(
                remote(
                    x.at[pl.ds(yt * ROWS, ROWS), :],
                    there,
                    bsend.at[i, d - 1],
                    brecv.at[i, d - 1],
                    z,
                    yt,
                )
            )
        copies.append(pltpu.make_async_copy(x.at[here, :], there, local.at[i]))
        for copy in copies:
            copy.start()
        kv_out.extend(copies)

    total = add_up(shared, gx, ndp)
    shared = share(gz, z, NZ, NY - 1, total, lambda to: {"context": to * NY + y})
    for h in range(2):
        back(0, 1, h).wait_recv()
        at = (lower, upper)[h]
        rows = slice(own + h * half, own + (h + 1) * half)
        raw = slice(2 * SLAB + h * half, 2 * SLAB + (h + 1) * half)
        dkt = (dk[rows, :] * SCALE + rk[1, at, :].astype(F32)).T
        dx, _ = norm_backward(
            kraw[raw, :].T.astype(F32), kgain_col, dkt, cos_buf[:, raw], sin_buf[:, raw]
        )
        kg[at, :] = dx.astype(BF16).T
    leave_row(0, kg, okg)
    total = add_up(shared, gz, NZ)
    shared = share(gy, y, NY, 0, total, lambda to: {"context": z * NY + to})
    for h in range(2):
        back(1, 1, h).wait_recv()
    vg[...] = (dv[own:, :] + rv[1].astype(F32)).astype(BF16)
    leave_row(1, vg, ovg)
    gains_out[...] = add_up(shared, gy, NY)[:2]

    for w in range(2):
        for d in hops:
            for copy in out_copies(w, d):
                copy.wait()
            for copy in query_copies(w, d):
                copy.wait_send()
        for copy in out_stays(w):
            copy.wait()
    leaving = [
        pltpu.make_async_copy(oa, attn_out, local.at[2]),
        pltpu.make_async_copy(oq, dq_out, local.at[3]),
    ]
    for copy in leaving:
        copy.start()
    for copy in kv_out:
        copy.wait()
    for i, (x, out) in enumerate(((okg, kg_out), (ovg, vg_out))):
        copy = pltpu.make_async_copy(x, out, local.at[4 + i])
        copy.start()
        leaving.append(copy)
    for copies in (ycopies, zcopies):
        for copy in copies.values():
            copy.wait_send()
    for i in range(2):
        for hop in range(2):
            for h in range(2):
                back(i, hop, h).wait_send()
    for copy in leaving:
        copy.wait()


def finish_kernel(*refs):
    n = (len(refs) - 1) // 3
    sems = refs[-1]
    into = [
        pltpu.make_async_copy(refs[i], refs[2 * n + i], sems.at[0, i]) for i in range(n)
    ]
    out = [
        pltpu.make_async_copy(refs[2 * n + i], refs[n + i], sems.at[1, i])
        for i in range(n)
    ]
    for copy in into:
        copy.start()
    for a, b in zip(into, out):
        a.wait()
        b.start()
    for copy in out:
        copy.wait()


VMEM = pl.BlockSpec(memory_space=pltpu.VMEM)
HBM = pl.BlockSpec(memory_space=pltpu.HBM)
ANY = pl.BlockSpec(memory_space=pl.ANY)
DMA = pltpu.SemaphoreType.DMA


def body(queries, keys, values, pkeys, pvalues, out_grad, query_gain, key_gain, lengths, offsets):
    ndp = lax.axis_size("dp")
    sd = jax.ShapeDtypeStruct

    def vmem(shape, dtype, count=1):
        return [pltpu.VMEM(shape, dtype)] * count

    def dma(shape, count=2):
        return [DMA(shape)] * count

    results = pl.pallas_call(
        functools.partial(fused_kernel, ndp),
        name="fused",
        out_shape=(
            sd((ROWS, NY * COLS), BF16),
            sd((ROWS, NY * COLS), BF16),
            sd((ROWS, NY * D), BF16),
            sd((ROWS, NY * D), BF16),
            sd((2, D), F32),
        ),
        in_specs=[HBM] * 2 + [VMEM] * 2 + [HBM] * 6,
        out_specs=(ANY, ANY, ANY, ANY, VMEM),
        scratch_shapes=vmem((SLAB, COLS), BF16, 2)
        + vmem((KEYS, D), BF16, 2)
        + vmem((D, KEYS), BF16, 2)
        + vmem((WINDOW, D), BF16)
        + vmem((D, WINDOW), F32)
        + vmem((HALF, WINDOW), F32, 2)
        + vmem((D, D), F32)
        + vmem((NY * MET, ROWS), F32)
        + vmem((D, HQ * SLAB), BF16, 3)
        + vmem((HQ * SLAB, D), BF16, 2)
        + vmem((2, MET, LANES), F32, 2)
        + vmem((MET, WIDE), BF16, 2)
        + vmem((KEYS, D), F32, 2)
        + vmem((D, ROWS), F32)
        + vmem((SLAB, COLS), BF16, 2)
        + vmem((ROWS, NY * COLS), BF16, 2)
        + vmem((ROWS, NY * D), BF16, 2)
        + vmem((2, SLAB, D), BF16, 2)
        + vmem((2, SLAB // 2, D), BF16, 2)
        + vmem((SLAB, D), BF16, 2)
        + vmem((NY, 8, D), F32)
        + vmem((NZ, 8, D), F32)
        + vmem((ndp, 8, D), F32)
        + [pltpu.SMEM((1, SEGS), jnp.int32)] * 2
        + dma((2,), 1)
        + dma((4, NY - 1))
        + dma((2, 2, NY - 1))
        + dma((2,))
        + dma((2, NY))
        + dma((2, NZ - 1))
        + dma((2, 2, NY - 1))
        + dma((2, NY - 1))
        + dma((2, 2, 2))
        + dma((NY + NZ + ndp - 3,))
        + dma((6,), 1)
        + dma((2, 2), 1),
        compiler_params=pltpu.CompilerParams(
            collective_id=0, has_side_effects=True, vmem_limit_bytes=62 << 20
        ),
    )(
        lengths,
        offsets,
        query_gain.reshape(1, D),
        key_gain.reshape(1, D),
        queries[0],
        out_grad[0],
        keys[0],
        values[0],
        pkeys[0],
        pvalues[0],
    )
    attention, query_grad, key_grad, value_grad, gains = pl.pallas_call(
        finish_kernel,
        name="finish",
        out_shape=[sd(x.shape, x.dtype) for x in results],
        in_specs=[ANY] * 5,
        out_specs=[HBM] * 5,
        scratch_shapes=[pltpu.VMEM(x.shape, x.dtype) for x in results] + [DMA((2, 5))],
        compiler_params=pltpu.CompilerParams(vmem_limit_bytes=62 << 20),
    )(*results)
    return attention[None], query_grad[None], key_grad[None], value_grad[None], gains


def solution(mesh):
    rows = P("dp", "context", None)
    in_specs = (rows,) * 6 + (P(), P(), P("dp", None), P("dp", None))
    out_specs = (rows,) * 4 + (P(),)
    return jax.shard_map(body, mesh=mesh, in_specs=in_specs, out_specs=out_specs, check_vma=False)
```

time: 922 us -> 78.1 us (0.08); the launches traced: 907 us -> 78 us
  waiting for transfers between devices: 304 us -> 0 us
  blocking collectives: 177 us -> 0 us
  local copies, waits for them, and re-layouts: 173 us -> 0 us
  other arithmetic: 133 us -> 0 us
  Pallas kernels: 0 us -> 77.4 us
  matrix products: 65 us -> 0 us
  starting transfers between devices: 34.3 us -> 0 us
  between operations: 14.9 us -> 0.64 us
    reduce_scatter x2 -> x0, waiting for transfers between devices: 284 us -> none  [the longest x1 144 us: body(): lax.psum_scatter(place_head(key_total).astype(jnp.bfloat16), 'context', s...]
    all_gather x2 -> x0, blocking collectives: 97.4 us -> none  [the longest x1 58.7 us: body(): lax.all_gather(prefix_cached_keys, 'context', axis=1, tiled=True)]
    unnamed x4 -> x0, other arithmetic: 93.2 us -> none
    psum x1 -> x0, blocking collectives: 79.9 us -> none  [body(): lax.psum(jnp.stack([query_gain_part, key_gain_part]), ('dp', 'context'))]
    pallas_call x0 -> x2, Pallas kernels: none -> 77.4 us  [the longest x1 74.7 us: body(): pl.pallas_call(functools.partial(fused_kernel, ndp), name='fused', out_sh...]
    dot_general x48 -> x0, matrix products: 65 us -> none  [the longest x8 14.8 us: block_step(): jnp.einsum('qhd,kd->hqk', grad_block, value_row_block, preferred_element_...]
    dynamic_update_slice x40 -> x0, local copies, waits for them, and re-layouts: 62.7 us -> none  [the longest x8 27.7 us: block_step(): lax.dynamic_update_slice_in_dim(value_total, lax.dynamic_slice_in_dim(val...]
    unnamed x70 -> x0, local copies, waits for them, and re-layouts: 38 us -> none
  transfers between devices with their start and end apart: 8 -> 0, of which waited for: 4 -> 0; matrix products, arithmetic and copies ran while one was open for 20% -> 0% of each run, Pallas kernels for 0% -> 0%
where the time goes in v1:
time: 78.1 us; the launch traced here: 78 us
  Pallas kernels  77.4 us (99%)
    pallas_call x1, Pallas kernels, body(): pl.pallas_call(functools.partial(fused_kernel, ndp), name='fused', out_sh...  74.7 us
    pallas_call x1, Pallas kernels, body(): pl.pallas_call(finish_kernel, name='finish', out_shape=[sd(x.shape, x.dty...  2.7 us

profile of v1, /device:TPU:1, one launch (start us, length us, event | category | flops | bytes accessed | tf_op | source)
XLA Modules:
  0.0 78.0 jit_solution(13980653530356041573)
XLA Ops:
  0.6 74.7 %fused.1 = (bf16[128,4096]{1,0:T(8,128)(2,1)}, bf16[128,4096]{1,0:T(8,128)(2,1)}, bf16[128,512]{1,0:T(8,128)(2,1)}, bf16[128,512]{1,0:T(8,128)(2,1)}, f32[2,128]{1,0:T(2,128)}) custom-call(s32[1,8]{1,0:T(1,128)} %lengths_in.1, s32[1,8]{1,0:T(1,128)} %offsets_in.1, f32[1,128]{1,0:T(1,128)} %bitcast.18, f32[1,128]{1,0:T(1,128)} %bitcast.19, ...), custom_call_target="tpu_custom_call" | custom-call | tf_op jit(solution)/shard_map/fused/pallas_call | solution.py:768
  75.3 2.7 %finish.1 = (bf16[128,4096]{1,0:T(8,128)(2,1)}, bf16[128,4096]{1,0:T(8,128)(2,1)}, bf16[128,512]{1,0:T(8,128)(2,1)}, bf16[128,512]{1,0:T(8,128)(2,1)}, f32[2,128]{1,0:T(2,128)}) custom-call(bf16[128,4096]{1,0:T(8,128)(2,1)} %get-tuple-element.15.refs_0_, bf16[128,4096]{1,0:T(8,128)(2,1)} %get-tuple-element.16.refs_1_, ...), custom_call_target="tpu_custom_call" | custom-call | tf_op jit(solution)/shard_map/finish/pallas_call | solution.py:831

commit v2 on v1

--- a/solution.py
+++ b/solution.py
@@ -428,6 +428,7 @@
             if i != 2:
                 zcopies[j, i, "cached"].wait_recv()
         xtr[:, :CACHE] = x[:CACHE, :].T
+    prepare(0, y)
     zcopies[0, "far"].wait_recv()
     rotate_keys(0)
     zcopies[1, "far"].wait_recv()
@@ -554,29 +555,41 @@
             for a, (x, buf) in enumerate(((oh, oa), (dqh, oq)))
         ]
 
+    d_last = jnp.where(y == 0, 3, jnp.where(y == 1, 1, 0))
+
+    def await_unit(w, d):
+        @pl.when(d > 0)
+        def _():
+            for copy in query_copies(w, NY - d):
+                copy.wait_recv()
+
+    def leave_unit(w, d):
+        @pl.when(d > 0)
+        def _():
+            for copy in out_copies(w, d):
+                copy.start()
+
+        @pl.when(d == 0)
+        def _():
+            for copy in out_stays(w):
+                copy.start()
+
     def step(n, carry):
         w = jnp.where((n == 3) | (n == 4) | (n == 6), 1, 0)
         d = jnp.where(n == 0, 0, jnp.where(n > 4, 2, jnp.where((n == 1) | (n == 3), 1, 3)))
+        d = jnp.where(((n == 3) | (n == 4)) & (d == d_last), 0, d)
         b = lax.rem(y + d, NY)
 
         @pl.when(n > 0)
         def _():
-            for copy in query_copies(w, NY - d):
-                copy.wait_recv()
-
-        prepare(w, b)
+            await_unit(w, d)
+            prepare(w, b)
+
         attend(w, b)
-
-        @pl.when(n > 0)
-        def _():
-            for copy in out_copies(w, d):
-                copy.start()
-
+        leave_unit(w, d)
         return carry
 
     lax.fori_loop(0, 7, step, 0)
-    for copy in out_stays(0):
-        copy.start()
 
     half = SLAB // 2
     lower, upper = slice(0, half), slice(half, SLAB)
@@ -609,14 +622,15 @@
             got[0, at, :] = mid.astype(BF16)
             back(i, 1, h).start()
 
-    prepare(1, y)
-    attend(1, y, True)
     first_hop(0)
+    b_last = lax.rem(y + d_last, NY)
+    await_unit(1, d_last)
+    prepare(1, b_last)
+    attend(1, b_last, True)
     first_hop(1)
-    rest(1, y)
-    for copy in out_stays(1):
-        copy.start()
     second_hop(0)
+    rest(1, b_last)
+    leave_unit(1, d_last)
 
     terms = jnp.zeros((D, ROWS), F32)
     for slab in range(3):
@@ -733,13 +747,16 @@
 def finish_kernel(*refs):
     n = (len(refs) - 1) // 3
     sems = refs[-1]
-    into = [
-        pltpu.make_async_copy(refs[i], refs[2 * n + i], sems.at[0, i]) for i in range(n)
-    ]
-    out = [
-        pltpu.make_async_copy(refs[2 * n + i], refs[n + i], sems.at[1, i])
-        for i in range(n)
-    ]
+    into, out = [], []
+    for i in range(n):
+        rows = refs[i].shape[0]
+        size = rows // 4 if i < 2 else rows
+        for first in range(0, rows, size):
+            at = pl.ds(first, size)
+            held = refs[2 * n + i].at[at, :]
+            sem = len(into)
+            into.append(pltpu.make_async_copy(refs[i].at[at, :], held, sems.at[0, sem]))
+            out.append(pltpu.make_async_copy(held, refs[n + i].at[at, :], sems.at[1, sem]))
     for copy in into:
         copy.start()
     for a, b in zip(into, out):
@@ -834,7 +851,7 @@
         out_shape=[sd(x.shape, x.dtype) for x in results],
         in_specs=[ANY] * 5,
         out_specs=[HBM] * 5,
-        scratch_shapes=[pltpu.VMEM(x.shape, x.dtype) for x in results] + [DMA((2, 5))],
+        scratch_shapes=[pltpu.VMEM(x.shape, x.dtype) for x in results] + [DMA((2, 11))],
         compiler_params=pltpu.CompilerParams(vmem_limit_bytes=62 << 20),
     )(*results)
     return attention[None], query_grad[None], key_grad[None], value_grad[None], gains

time: 78.1 us -> 76.2 us (0.976)
  Pallas kernels: 77.4 us -> 75.4 us
    pallas_call x1, Pallas kernels: 74.7 us -> 72.9 us  [body(): pl.pallas_call(functools.partial(fused_kernel, ndp), name='fused', out_sh...]
where the time goes in v2:
time: 76.2 us; the launch traced here: 76 us
  Pallas kernels  75.4 us (99%)
    pallas_call x1, Pallas kernels, body(): pl.pallas_call(functools.partial(fused_kernel, ndp), name='fused', out_sh...  72.9 us
    pallas_call x1, Pallas kernels, body(): pl.pallas_call(finish_kernel, name='finish', out_shape=[sd(x.shape, x.dty...  2.53 us

profile of v2, /device:TPU:1, one launch (start us, length us, event | category | flops | bytes accessed | tf_op | source)
XLA Modules:
  0.0 76.0 jit_solution(12840528210921521874)
XLA Ops:
  0.6 72.9 %fused.1 = (bf16[128,4096]{1,0:T(8,128)(2,1)}, bf16[128,4096]{1,0:T(8,128)(2,1)}, bf16[128,512]{1,0:T(8,128)(2,1)}, bf16[128,512]{1,0:T(8,128)(2,1)}, f32[2,128]{1,0:T(2,128)}) custom-call(s32[1,8]{1,0:T(1,128)} %lengths_in.1, s32[1,8]{1,0:T(1,128)} %offsets_in.1, f32[1,128]{1,0:T(1,128)} %bitcast.18, f32[1,128]{1,0:T(1,128)} %bitcast.19, ...), custom_call_target="tpu_custom_call" | custom-call | tf_op jit(solution)/shard_map/fused/pallas_call | solution.py:785
  73.5 2.5 %finish.1 = (bf16[128,4096]{1,0:T(8,128)(2,1)}, bf16[128,4096]{1,0:T(8,128)(2,1)}, bf16[128,512]{1,0:T(8,128)(2,1)}, bf16[128,512]{1,0:T(8,128)(2,1)}, f32[2,128]{1,0:T(2,128)}) custom-call(bf16[128,4096]{1,0:T(8,128)(2,1)} %get-tuple-element.15.refs_0_, bf16[128,4096]{1,0:T(8,128)(2,1)} %get-tuple-element.16.refs_1_, ...), custom_call_target="tpu_custom_call" | custom-call | tf_op jit(solution)/shard_map/finish/pallas_call | solution.py:848

commit v3 on v2

--- a/solution.py
+++ b/solution.py
@@ -293,7 +293,7 @@
 
     for copy in mine_q:
         copy.start()
-    send_queries(((0, 3), (0, 1)))
+    send_queries(((0, 3), (0, 1), (1, 3), (1, 1)))
 
     for copy in pieces:
         copy.wait()
@@ -358,15 +358,18 @@
         copy.start()
         zcopies[j, i, "cached"] = copy
 
+    def pass_next(j):
+        for d in range(NY):
+            zcopies[j, d, "next"].wait_recv()
+        forward(j)
+
+    pass_next(0)
     for j in range(2):
         arrived(2 + j)
         for i, d in enumerate((1, 2, 5, 6, 7)):
             cached_to(j, i, pl.ds(crow, NY * CPART), d)
-    for j in range(2):
-        for d in range(NY):
-            zcopies[j, d, "next"].wait_recv()
-        forward(j)
-    send_queries(((1, 3), (1, 1), (0, 2), (1, 2)))
+    pass_next(1)
+    send_queries(((0, 2), (1, 2)))
 
     def mask(b, carry):
         t = z * SLAB + b * ROWS + lax.broadcasted_iota(jnp.int32, (1, ROWS), 1)
@@ -668,8 +671,8 @@
             total = total + buf[i]
         return total
 
+    shared = share(gx, dp, ndp, NY + NZ - 2, total, lambda to: {"dp": to})
     second_hop(1)
-    shared = share(gx, dp, ndp, NY + NZ - 2, total, lambda to: {"dp": to})
     kv_out = []
 
     def leave_row(i, x, buf):
@@ -711,7 +714,6 @@
         back(1, 1, h).wait_recv()
     vg[...] = (dv[own:, :] + rv[1].astype(F32)).astype(BF16)
     leave_row(1, vg, ovg)
-    gains_out[...] = add_up(shared, gy, NY)[:2]
 
     for w in range(2):
         for d in hops:
@@ -727,6 +729,7 @@
     ]
     for copy in leaving:
         copy.start()
+    gains_out[...] = add_up(shared, gy, NY)[:2]
     for copy in kv_out:
         copy.wait()
     for i, (x, out) in enumerate(((okg, kg_out), (ovg, vg_out))):

time: 76.2 us -> 76.1 us (level)
  no operation moved by 1% of the time
where the time goes in v3:
time: 76.1 us; the launch traced here: 76 us
  Pallas kernels  75.3 us (99%)
    pallas_call x1, Pallas kernels, body(): pl.pallas_call(functools.partial(fused_kernel, ndp), name='fused', out_sh...  72.8 us
    pallas_call x1, Pallas kernels, body(): pl.pallas_call(finish_kernel, name='finish', out_shape=[sd(x.shape, x.dty...  2.53 us

profile of v3, /device:TPU:1, one launch (start us, length us, event | category | flops | bytes accessed | tf_op | source)
XLA Modules:
  0.0 76.0 jit_solution(8559875310892025460)
XLA Ops:
  0.6 72.8 %fused.1 = (bf16[128,4096]{1,0:T(8,128)(2,1)}, bf16[128,4096]{1,0:T(8,128)(2,1)}, bf16[128,512]{1,0:T(8,128)(2,1)}, bf16[128,512]{1,0:T(8,128)(2,1)}, f32[2,128]{1,0:T(2,128)}) custom-call(s32[1,8]{1,0:T(1,128)} %lengths_in.1, s32[1,8]{1,0:T(1,128)} %offsets_in.1, f32[1,128]{1,0:T(1,128)} %bitcast.18, f32[1,128]{1,0:T(1,128)} %bitcast.19, ...), custom_call_target="tpu_custom_call" | custom-call | tf_op jit(solution)/shard_map/fused/pallas_call | solution.py:788
  73.5 2.5 %finish.1 = (bf16[128,4096]{1,0:T(8,128)(2,1)}, bf16[128,4096]{1,0:T(8,128)(2,1)}, bf16[128,512]{1,0:T(8,128)(2,1)}, bf16[128,512]{1,0:T(8,128)(2,1)}, f32[2,128]{1,0:T(2,128)}) custom-call(bf16[128,4096]{1,0:T(8,128)(2,1)} %get-tuple-element.15.refs_0_, bf16[128,4096]{1,0:T(8,128)(2,1)} %get-tuple-element.16.refs_1_, ...), custom_call_target="tpu_custom_call" | custom-call | tf_op jit(solution)/shard_map/finish/pallas_call | solution.py:851
